TPU v7x, 32 devices: a whole 2x2x4 slice. The times are simulated.
32 devices in a mesh: psg: 16 (over z, y, core), row: 2 (over x).
Axes of the slice: x: 2, y: 2, z: 4, core: 2. Of those that a mesh axis runs over, the one named last changes fastest.
Arguments:
- psg_len: int32 [32], P('psg'), may hold values from 128 to 512, as said below
- offsets: int32 [32], P('psg'), may hold values from 0 to 1023
- p_query: bfloat16 [32, 512, 8192], P('psg', None, 'row'), may hold values from -8 to 8
- passage_key: bfloat16 [32, 512, 1024], P('psg', None, 'row'), may hold values from -8 to 8
- passage_value: bfloat16 [32, 512, 1024], P('psg', None, 'row'), may hold values from -6 to 6
- p_grad: bfloat16 [32, 512, 8192], P('psg', None, 'row'), may hold values from -6 to 6
- a_query: bfloat16 [64, 8192], P('row'), may hold values from -8 to 8
- a_grad: bfloat16 [64, 8192], P('row'), may hold values from -6 to 6
Outputs:
- p_out: bfloat16 [32, 512, 8192], P('psg', None, 'row')
- p_dq: bfloat16 [32, 512, 8192], P('psg', None, 'row')
- p_dk: bfloat16 [32, 512, 1024], P('psg', None, 'row')
- p_dv: bfloat16 [32, 512, 1024], P('psg', None, 'row')
- a_out: bfloat16 [64, 8192], P('row')
- a_dq: bfloat16 [64, 8192], P('row')
Inputs may be any that keep to these rules, and one draw needn't show every extreme that they name: `psg_len`: in every draw some passage holds exactly 512 tokens; a passage's tokens fill its first slots.
All inputs are finite; a program needn't handle non-finite values.
Results may differ from a plain program's by a relative error of at most 0.024.
Values may be sent and summed in bfloat16 or wider, within the bound.
A program may use at most 256 MiB of HBM per device.

v0:
```python
import functools
import math

import jax
import jax.numpy as jnp
from jax import lax
from jax.experimental import pallas as pl
from jax.experimental.pallas import tpu as pltpu
from jax.sharding import PartitionSpec as P

HEAD_SIZE = 128
ROPE_BASE = 500000.0
SCALE_FACTOR = 8.0
LOW_FACTOR = 1.0
HIGH_FACTOR = 4.0
OLD_CONTEXT = 8192.0
FILL_VALUE = -1e30
LOG2E = math.log2(math.e)
SCALE = 1.0 / math.sqrt(HEAD_SIZE)
BLOCK = 128
F32 = jnp.float32
BF16 = jnp.bfloat16
VMEM_LIMIT = 50 * 1024 * 1024


def rope_freq(half_dim):
    step_index = jnp.arange(half_dim, dtype=F32)
    base_freq = jnp.exp(step_index * (-math.log(ROPE_BASE) / half_dim))
    wavelength = 2.0 * math.pi / base_freq
    smooth = (OLD_CONTEXT / wavelength - LOW_FACTOR) / (HIGH_FACTOR - LOW_FACTOR)
    blended = (1.0 - smooth) * base_freq / SCALE_FACTOR + smooth * base_freq
    return jnp.where(
        wavelength < OLD_CONTEXT / HIGH_FACTOR,
        base_freq,
        jnp.where(wavelength > OLD_CONTEXT / LOW_FACTOR, base_freq / SCALE_FACTOR, blended),
    )


def mm_nt(a, b):
    return lax.dot_general(a, b, (((1,), (1,)), ((), ())), preferred_element_type=F32)


def mm(a, b):
    return lax.dot_general(a, b, (((1,), (0,)), ((), ())), preferred_element_type=F32)


def head_stack(ref_rows, heads):
    return jnp.concatenate([ref_rows(h) for h in heads], axis=0)


def passage_kernel(first, adds, len_ref, q_ref, k_ref, v_ref, g_ref, *rest):
    if adds:
        ak_ref, av_ref = rest[:2]
    o_ref, dq_ref, dk_ref, dv_ref, dk_acc, dv_acc = rest[-6:]
    slots = k_ref.shape[1]
    groups = q_ref.shape[2] // HEAD_SIZE
    length = len_ref[first + pl.program_id(0)]
    key = k_ref[0]
    val = v_ref[0]
    key_t = key.T
    val_t = val.T
    if adds:
        dk_acc[...] = ak_ref[0]
        dv_acc[...] = av_ref[0]
    else:
        dk_acc[...] = jnp.zeros_like(dk_acc)
        dv_acc[...] = jnp.zeros_like(dv_acc)
    width = 2 * BLOCK
    causal = lax.broadcasted_iota(jnp.int32, (BLOCK, width), 0) <= (
        lax.broadcasted_iota(jnp.int32, (BLOCK, width), 1) & (BLOCK - 1)
    )
    lane_pos = lax.broadcasted_iota(jnp.int32, (1, width), 1) & (BLOCK - 1)
    row_pos = lax.broadcasted_iota(jnp.int32, (width, HEAD_SIZE), 0) & (BLOCK - 1)
    for b in range(slots // BLOCK):
        lo = b * BLOCK
        hi = lo + BLOCK

        @pl.when(length <= lo)
        def _():
            o_ref[0, lo:hi, :] = jnp.zeros((BLOCK, o_ref.shape[2]), BF16)
            dq_ref[0, lo:hi, :] = jnp.zeros((BLOCK, o_ref.shape[2]), BF16)

        @pl.when(length > lo)
        def _():
            row_ok = row_pos + lo < length
            lane_ok = lane_pos + lo < length
            qs, gs, ps, dss = [], [], [], []
            for h in range(0, groups, 2):
                heads = (h, h + 1)
                q2 = head_stack(lambda x: q_ref[0, lo:hi, x * HEAD_SIZE : (x + 1) * HEAD_SIZE], heads)
                g2 = head_stack(lambda x: g_ref[0, lo:hi, x * HEAD_SIZE : (x + 1) * HEAD_SIZE], heads)
                g2 = jnp.where(row_ok, g2.astype(F32), 0.0).astype(BF16)
                s = mm_nt(key[:hi], q2)
                tail = jnp.where(causal, s[lo:], FILL_VALUE)
                s = tail if b == 0 else jnp.concatenate([s[:lo], tail], axis=0)
                s = s * (SCALE * LOG2E)
                m = jnp.max(s, axis=0, keepdims=True)
                e = jnp.exp2(s - m)
                p = e * (1.0 / jnp.sum(e, axis=0, keepdims=True))
                pb = p.astype(BF16)
                dp = mm_nt(val[:hi], g2)
                delta = jnp.sum(p * dp, axis=0, keepdims=True)
                ds = (p * (dp - delta)).astype(BF16)
                o = jnp.where(lane_ok, mm(val_t[:, :hi], pb), 0.0).T.astype(BF16)
                dq = (mm(key_t[:, :hi], ds) * SCALE).T.astype(BF16)
                for n, x in enumerate(heads):
                    cols = slice(x * HEAD_SIZE, (x + 1) * HEAD_SIZE)
                    o_ref[0, lo:hi, cols] = o[n * BLOCK : (n + 1) * BLOCK]
                    dq_ref[0, lo:hi, cols] = dq[n * BLOCK : (n + 1) * BLOCK]
                qs.append(q2)
                gs.append(g2)
                ps.append(pb)
                dss.append(ds)
            dk_acc[:hi] += mm(jnp.concatenate(dss, axis=1), jnp.concatenate(qs, axis=0)) * SCALE
            dv_acc[:hi] += mm(jnp.concatenate(ps, axis=1), jnp.concatenate(gs, axis=0))

    dk_ref[0] = dk_acc[...].astype(dk_ref.dtype)
    dv_ref[0] = dv_acc[...].astype(dv_ref.dtype)


def run_passages(lengths, query, key, val, grad):
    count, slots, feat = query.shape
    kv = key.shape[2] // HEAD_SIZE
    group_width = feat // kv
    wide = pl.BlockSpec((1, slots, group_width), lambda p, g: (p, 0, g))
    thin = pl.BlockSpec((1, slots, HEAD_SIZE), lambda p, g: (p, 0, g))
    return pl.pallas_call(
        functools.partial(passage_kernel, 0, False),
        grid=(count, kv),
        in_specs=[pl.BlockSpec(memory_space=pltpu.SMEM), wide, thin, thin, wide],
        out_specs=[wide, wide, thin, thin],
        out_shape=[
            jax.ShapeDtypeStruct(query.shape, BF16),
            jax.ShapeDtypeStruct(query.shape, BF16),
            jax.ShapeDtypeStruct(key.shape, F32),
            jax.ShapeDtypeStruct(key.shape, F32),
        ],
        scratch_shapes=[pltpu.VMEM((slots, HEAD_SIZE), F32)] * 2,
        compiler_params=pltpu.CompilerParams(vmem_limit_bytes=VMEM_LIMIT),
        cost_estimate=pl.CostEstimate(
            flops=8 * count * slots * slots * feat,
            bytes_accessed=8 * count * slots * feat,
            transcendentals=count * slots * slots * feat // HEAD_SIZE,
        ),
        name="passages",
    )(lengths, query, key, val, grad)


def rotated(key, cos, sin):
    wide = key.astype(F32)
    return (wide * cos + pltpu.roll(wide, HEAD_SIZE // 2, 1) * sin).astype(BF16)


def chunk_heads(tokens):
    return max(1, 256 // tokens)


def stats_kernel(len_ref, cos_ref, sin_ref, q_ref, g_ref, k_ref, v_ref, out_ref):
    count, slots = k_ref.shape[:2]
    tokens = q_ref.shape[0]
    groups = q_ref.shape[1] // HEAD_SIZE
    step = chunk_heads(tokens)
    keys = [rotated(k_ref[p], cos_ref[p], sin_ref[p]) for p in range(count)]
    at = lax.broadcasted_iota(jnp.int32, (slots, step * tokens), 0)
    for h in range(0, groups, step):
        heads = range(h, h + step)
        q2 = head_stack(lambda x: q_ref[:, x * HEAD_SIZE : (x + 1) * HEAD_SIZE], heads)
        g2 = head_stack(lambda x: g_ref[:, x * HEAD_SIZE : (x + 1) * HEAD_SIZE], heads)
        lses, deltas = [], []
        for p in range(count):
            s = mm_nt(keys[p], q2)
            s = jnp.where(at < len_ref[p], s, FILL_VALUE) * (SCALE * LOG2E)
            m = jnp.max(s, axis=0, keepdims=True)
            e = jnp.exp2(s - m)
            total = jnp.sum(e, axis=0, keepdims=True)
            dp = mm_nt(v_ref[p], g2)
            lses.append(m + jnp.log2(total))
            deltas.append(jnp.sum(e * dp, axis=0, keepdims=True) / total)
        lse, delta = merge(jnp.concatenate(lses, axis=0), jnp.concatenate(deltas, axis=0))
        cols = slice(h * tokens, (h + step) * tokens)
        out_ref[0, 0:1, cols] = lse
        out_ref[0, 1:2, cols] = delta


def merge(lses, deltas):
    m = jnp.max(lses, axis=0, keepdims=True)
    w = jnp.exp2(lses - m)
    total = jnp.sum(w, axis=0, keepdims=True)
    return m + jnp.log2(total), jnp.sum(w * deltas, axis=0, keepdims=True) / total


def run_stats(lengths, cos, sin, query, grad, key, val):
    count, slots, feat = key.shape
    kv = feat // HEAD_SIZE
    tokens, width = query.shape
    groups = width // feat
    wide = pl.BlockSpec((tokens, width // kv), lambda g: (0, g))
    thin = pl.BlockSpec((count, slots, HEAD_SIZE), lambda g: (0, 0, g))
    whole = pl.BlockSpec((count, 1, HEAD_SIZE), lambda g: (0, 0, 0))
    return pl.pallas_call(
        stats_kernel,
        grid=(kv,),
        in_specs=[pl.BlockSpec(memory_space=pltpu.SMEM), whole, whole, wide, wide, thin, thin],
        out_specs=pl.BlockSpec((1, 2, groups * tokens), lambda g: (g, 0, 0)),
        out_shape=jax.ShapeDtypeStruct((kv, 2, groups * tokens), F32),
        compiler_params=pltpu.CompilerParams(vmem_limit_bytes=VMEM_LIMIT),
        cost_estimate=pl.CostEstimate(
            flops=4 * count * slots * tokens * width,
            bytes_accessed=4 * count * slots * feat + 4 * tokens * width,
            transcendentals=count * slots * tokens * groups * kv,
        ),
        name="answer_stats",
    )(lengths, cos, sin, query, grad, key, val)


def grads_kernel(
    len_ref, cos_ref, sin_ref, q_ref, g_ref, k_ref, v_ref, stat_ref, pk_ref, pv_ref,
    o_ref, dq_ref, dk_ref, dv_ref, dk_acc, dv_acc,
):
    count, slots = k_ref.shape[:2]
    tokens = q_ref.shape[0]
    groups = q_ref.shape[1] // HEAD_SIZE
    step = chunk_heads(tokens)
    keys = [rotated(k_ref[p], cos_ref[p], sin_ref[p]) for p in range(count)]
    keys_t = [k.T for k in keys]
    vals_t = [v_ref[p].T for p in range(count)]
    at = lax.broadcasted_iota(jnp.int32, (slots, step * tokens), 0)
    for h in range(0, groups, step):
        heads = range(h, h + step)
        cols = slice(h * tokens, (h + step) * tokens)
        q2 = head_stack(lambda x: q_ref[:, x * HEAD_SIZE : (x + 1) * HEAD_SIZE], heads)
        g2 = head_stack(lambda x: g_ref[:, x * HEAD_SIZE : (x + 1) * HEAD_SIZE], heads)
        lse, delta = merge(stat_ref[:, 0, 0, cols], stat_ref[:, 0, 1, cols])
        o_t = dq_t = None
        for p in range(count):
            s = mm_nt(keys[p], q2) * (SCALE * LOG2E)
            prob = jnp.where(at < len_ref[p], jnp.exp2(s - lse), 0.0)
            pb = prob.astype(BF16)
            dp = mm_nt(v_ref[p], g2)
            ds = (prob * (dp - delta)).astype(BF16)
            o_new = mm(vals_t[p], pb)
            dq_new = mm(keys_t[p], ds)
            o_t = o_new if p == 0 else o_t + o_new
            dq_t = dq_new if p == 0 else dq_t + dq_new
            dk_new = mm(ds, q2)
            dv_new = mm(pb, g2)
            if h == 0:
                dk_acc[p] = dk_new
                dv_acc[p] = dv_new
            else:
                dk_acc[p] += dk_new
                dv_acc[p] += dv_new
        o = o_t.T.astype(BF16)
        dq = (dq_t * SCALE).T.astype(BF16)
        for n, x in enumerate(heads):
            out_cols = slice(x * HEAD_SIZE, (x + 1) * HEAD_SIZE)
            o_ref[:, out_cols] = o[n * tokens : (n + 1) * tokens]
            dq_ref[:, out_cols] = dq[n * tokens : (n + 1) * tokens]
    for p in range(count):
        dk = dk_acc[p] * SCALE
        dk = dk * cos_ref[p] - pltpu.roll(dk, HEAD_SIZE // 2, 1) * sin_ref[p]
        dk_ref[p] = (dk + pk_ref[p]).astype(dk_ref.dtype)
        dv_ref[p] = (dv_acc[p] + pv_ref[p]).astype(dv_ref.dtype)


def run_grads(lengths, cos, sin, query, grad, key, val, stats, pass_dk, pass_dv):
    count, slots, feat = key.shape
    kv = feat // HEAD_SIZE
    tokens, width = query.shape
    groups = width // feat
    wide = pl.BlockSpec((tokens, width // kv), lambda g: (0, g))
    thin = pl.BlockSpec((count, slots, HEAD_SIZE), lambda g: (0, 0, g))
    whole = pl.BlockSpec((count, 1, HEAD_SIZE), lambda g: (0, 0, 0))
    stat = pl.BlockSpec((stats.shape[0], 1, 2, groups * tokens), lambda g: (0, g, 0, 0))
    return pl.pallas_call(
        grads_kernel,
        grid=(kv,),
        in_specs=[
            pl.BlockSpec(memory_space=pltpu.SMEM),
            whole, whole, wide, wide, thin, thin, stat, thin, thin,
        ],
        out_specs=[wide, wide, thin, thin],
        out_shape=[
            jax.ShapeDtypeStruct(query.shape, BF16),
            jax.ShapeDtypeStruct(query.shape, BF16),
            jax.ShapeDtypeStruct(key.shape, BF16),
            jax.ShapeDtypeStruct(key.shape, BF16),
        ],
        scratch_shapes=[pltpu.VMEM((count, slots, HEAD_SIZE), F32)] * 2,
        compiler_params=pltpu.CompilerParams(vmem_limit_bytes=VMEM_LIMIT),
        cost_estimate=pl.CostEstimate(
            flops=12 * count * slots * tokens * width,
            bytes_accessed=16 * count * slots * feat + 8 * tokens * width,
            transcendentals=count * slots * tokens * groups * kv,
        ),
        name="answer_grads",
    )(lengths, cos, sin, query, grad, key, val, stats, pass_dk, pass_dv)


def shards(n_psg, n_row, psg_len, offsets, p_query, passage_key, passage_value, p_grad, a_query, a_grad):
    def to_groups(rows):
        got = lax.all_to_all(rows, "row", split_axis=1, concat_axis=0, tiled=True)
        got = got.reshape(n_row, n_psg, -1, got.shape[1])
        return jnp.transpose(got, (1, 0, 2, 3)).reshape(-1, got.shape[3])

    queries = to_groups(a_query)
    grads_in = to_groups(a_grad)
    tokens, width = queries.shape
    share = tokens // (n_psg * n_row)

    angles = offsets.astype(F32)[:, None, None] * rope_freq(HEAD_SIZE // 2)
    cos = jnp.cos(angles)
    sin = jnp.sin(angles)
    cos = jnp.concatenate([cos, cos], axis=-1)
    sin = jnp.concatenate([-sin, sin], axis=-1)

    stats = run_stats(psg_len, cos, sin, queries, grads_in, passage_key, passage_value)
    stats = lax.all_gather(stats, "psg", axis=0)
    p_out, p_dq, pass_dk, pass_dv = run_passages(
        psg_len, p_query, passage_key, passage_value, p_grad
    )
    o_part, dq_part, p_dk, p_dv = run_grads(
        psg_len, cos, sin, queries, grads_in, passage_key, passage_value, stats, pass_dk, pass_dv
    )

    def to_owners(part):
        got = lax.all_to_all(part, ("psg", "row"), split_axis=0, concat_axis=0, tiled=True)
        got = got.reshape(n_psg, n_row, share, width).astype(F32)
        return jnp.sum(got, axis=0).astype(BF16)

    both = jnp.stack([to_owners(o_part), to_owners(dq_part)])
    both = jnp.transpose(both, (0, 2, 1, 3)).reshape(2, share, n_row * width)
    both = lax.all_gather(both, "psg", axis=1, tiled=True)
    return (p_out, p_dq, p_dk, p_dv, both[0], both[1])


def solution(mesh):
    return jax.shard_map(
        functools.partial(shards, mesh.shape["psg"], mesh.shape["row"]),
        mesh=mesh,
        in_specs=(
            P("psg"),
            P("psg"),
            P("psg", None, "row"),
            P("psg", None, "row"),
            P("psg", None, "row"),
            P("psg", None, "row"),
            P("row", None),
            P("row", None),
        ),
        out_specs=(
            P("psg", None, "row"),
            P("psg", None, "row"),
            P("psg", None, "row"),
            P("psg", None, "row"),
            P("row", None),
            P("row", None),
        ),
        check_vma=False,
    )
```

profile of v0, /device:TPU:0, one launch (start us, length us, event | category | flops | bytes accessed | tf_op | source)
XLA Modules:
  0.0 226.7 jit_solution(17590768747327008983)
XLA Ops:
  7.2 1.9 copy.38
  9.0 4.2 %all-to-all-start = ((bf16[32,2,4096]{2,0,1:T(8,128)(2,1)}), bf16[32,2,4096]{2,0,1:T(8,128)(2,1)S(1)}, u32[]{:S(2)}, u32[]{:S(2)}) async-start(bf16[32,2,4096]{2,0,1:T(8,128)(2,1)} %bitcast.27), calls=%async_computation | async-start | bytes 1048576 | tf_op jit(solution)/shard_map/all_to_all | solution.py:302
  13.2 1.2 copy-done
  14.5 1.2 copy-done.2
  15.7 0.7 copy-done.4
  16.4 41.4 %passages.1 = (bf16[2,512,4096]{2,1,0:T(8,128)(2,1)}, bf16[2,512,4096]{2,1,0:T(8,128)(2,1)}, f32[2,512,512]{2,1,0:T(8,128)}, f32[2,512,512]{2,1,0:T(8,128)}) custom-call(s32[2]{0:T(128)S(1)} %copy-done.4, bf16[2,512,4096]{2,1,0:T(8,128)(2,1)} %q_ref.1, bf16[2,512,512]{2,1,0:T(8,128)(2,1)S(1)} %copy-done, bf16[2,512,512]{2,1,0:T(8,128)(2,1)S(1)} %copy-done.2, ...), custom_call_target="tpu_custom_call" | custom-call | flops 17179869184 | bytes 33554432 | tf_op jit(solution)/shard_map/passages/pallas_call | solution.py:127
  57.8 0.8 copy.37
  58.6 3.7 %all-to-all-start.1 = ((bf16[32,2,4096]{2,0,1:T(8,128)(2,1)}), bf16[32,2,4096]{2,0,1:T(8,128)(2,1)S(1)}, u32[]{:S(2)}, u32[]{:S(2)}) async-start(bf16[32,2,4096]{2,0,1:T(8,128)(2,1)} %bitcast.26), calls=%async_computation.1 | async-start | bytes 1048576 | tf_op jit(solution)/shard_map/all_to_all | solution.py:302
  63.8 5.3 %all-to-all-done.1 = bf16[32,2,4096]{2,0,1:T(8,128)(2,1)S(1)} async-done(((bf16[32,2,4096]{2,0,1:T(8,128)(2,1)}), bf16[32,2,4096]{2,0,1:T(8,128)(2,1)S(1)}, u32[]{:S(2)}, u32[]{:S(2)}) %all-to-all-start.1) | async-done | bytes 524320 | tf_op jit(solution)/shard_map/all_to_all | solution.py:302
  70.4 1.2 copy-done.3
  71.6 5.3 %answer_stats.1 = f32[4,2,512]{2,1,0:T(2,128)S(1)} custom-call(s32[2]{0:T(128)S(1)} %copy-done.5, f32[2,1,128]{2,1,0:T(1,128)S(1)} %get-tuple-element.27.cos_ref, f32[2,1,128]{2,1,0:T(1,128)S(1)} %get-tuple-element.28.sin_ref, bf16[64,4096]{1,0:T(8,128)(2,1)S(1)} %reshape.195.q_ref, bf16[64,4096]{1,0:T(8,128)(2,1)S(1)} %reshape.197.g_ref, ...), custom_call_target="tpu_custom_call" | custom-call | flops 1073741824 | bytes 3145728 | tf_op jit(solution)/shard_map/answer_stats/pallas_call | solution.py:200
  76.9 50.4 %all-gather = f32[64,2,512]{2,1,0:T(2,128)S(1)} all-gather(f32[4,2,512]{2,1,0:T(2,128)S(1)} %answer_stats.1), channel_id=2, replica_groups=mesh['psg'=16,'row'=2] {'psg'}, dimensions={0}, use_global_device_ids=true | all-gather | bytes 278528 | tf_op jit(solution)/shard_map/all_gather | solution.py:318
  127.3 10.3 %answer_grads.1 = (bf16[64,4096]{1,0:T(8,128)(2,1)S(1)}, bf16[64,4096]{1,0:T(8,128)(2,1)S(1)}, bf16[2,512,512]{2,1,0:T(8,128)(2,1)}, bf16[2,512,512]{2,1,0:T(8,128)(2,1)}) custom-call(s32[2]{0:T(128)S(1)} %copy-done.5, f32[2,1,128]{2,1,0:T(1,128)S(1)} %get-tuple-element.27.cos_ref, f32[2,1,128]{2,1,0:T(1,128)S(1)} %get-tuple-element.28.sin_ref, ...), custom_call_target="tpu_custom_call" | custom-call | flops 3221225472 | bytes 10485760 | tf_op jit(solution)/shard_map/answer_grads/pallas_call | solution.py:275
  137.6 1.1 all_to_all.42
  138.8 2.6 %all-to-all-start.2 = ((bf16[32,2,4096]{2,1,0:T(2,128)(2,1)}), bf16[32,2,4096]{2,1,0:T(2,128)(2,1)S(1)}, u32[]{:S(2)}, u32[]{:S(2)}) async-start(bf16[32,2,4096]{2,1,0:T(2,128)(2,1)} %all_to_all.42), calls=%async_computation.2 | async-start | bytes 1048576 | tf_op jit(solution)/shard_map/all_to_all | solution.py:327
  141.4 1.1 all_to_all.44
  142.5 13.8 %all-to-all-done.2 = bf16[32,2,4096]{2,1,0:T(2,128)(2,1)S(1)} async-done(((bf16[32,2,4096]{2,1,0:T(2,128)(2,1)}), bf16[32,2,4096]{2,1,0:T(2,128)(2,1)S(1)}, u32[]{:S(2)}, u32[]{:S(2)}) %all-to-all-start.2) | async-done | bytes 524320 | tf_op jit(solution)/shard_map/all_to_all | solution.py:327
  156.4 3.5 %all-to-all-start.3 = ((bf16[32,2,4096]{2,1,0:T(2,128)(2,1)}), bf16[32,2,4096]{2,1,0:T(2,128)(2,1)S(1)}, u32[]{:S(2)}, u32[]{:S(2)}) async-start(bf16[32,2,4096]{2,1,0:T(2,128)(2,1)} %all_to_all.44), calls=%async_computation.3 | async-start | bytes 1048576 | tf_op jit(solution)/shard_map/all_to_all | solution.py:327
  160.4 14.5 %all-to-all-done.3 = bf16[32,2,4096]{2,1,0:T(2,128)(2,1)S(1)} async-done(((bf16[32,2,4096]{2,1,0:T(2,128)(2,1)}), bf16[32,2,4096]{2,1,0:T(2,128)(2,1)S(1)}, u32[]{:S(2)}, u32[]{:S(2)}) %all-to-all-start.3) | async-done | bytes 524320 | tf_op jit(solution)/shard_map/all_to_all | solution.py:327
  175.5 0.7 copy.26
  176.2 37.1 %all-gather.3.cloned.1.call-done = bf16[2,32,8192]{2,0,1:T(2,128)(2,1)} async-done(((bf16[2,2,8192]{2,0,1:T(2,128)(2,1)}), bf16[2,32,8192]{2,0,1:T(2,128)(2,1)}) %all-gather.3.cloned.1.call-update) | async-done | bytes 1048592 | tf_op jit(solution)/shard_map/all_gather | solution.py:333
  213.3 3.7 %fusion.1 = (bf16[1,32,8192]{2,0,1:T(2,128)(2,1)S(1)}, bf16[1,32,8192]{2,0,1:T(2,128)(2,1)S(1)}) fusion(bf16[2,32,8192]{2,0,1:T(2,128)(2,1)} %all-gather.3.cloned.1.call-done), kind=kLoop, calls=%fused_computation.12 | loop fusion | bytes 2097152 | tf_op jit(solution)/shard_map/slice | solution.py:334
  217.1 1.4 copy.39
  218.4 1.4 copy.40
  (28 shorter events, 3.9 us)
Async XLA Ops:
  9.0 49.6 %all-to-all-start = ((bf16[32,2,4096]{2,0,1:T(8,128)(2,1)}), bf16[32,2,4096]{2,0,1:T(8,128)(2,1)S(1)}, u32[]{:S(2)}, u32[]{:S(2)}) async-start(bf16[32,2,4096]{2,0,1:T(8,128)(2,1)} %bitcast.27), calls=%async_computation | async-start | bytes 1048576 | tf_op jit(solution)/shard_map/all_to_all | solution.py:302
  13.2 1.2 copy-start
  14.5 1.2 copy-start.2
  15.7 0.7 copy-start.4
  16.3 41.4 %copy-start.7 = (s32[2]{0:T(128)S(1)}, s32[2]{0:T(128)}, u32[]{:S(2)}) copy-start(s32[2]{0:T(128)} %param.9) | copy-start | bytes 28
  16.3 41.4 %copy-start.6 = (bf16[32,8192]{1,0:T(8,128)(2,1)S(1)}, bf16[32,8192]{1,0:T(8,128)(2,1)}, u32[]{:S(2)}) copy-start(bf16[32,8192]{1,0:T(8,128)(2,1)} %param.15) | copy-start | bytes 1572868
  57.7 12.7 %copy-start.1 = (bf16[2,512,512]{2,1,0:T(8,128)(2,1)S(1)}, bf16[2,512,512]{2,1,0:T(8,128)(2,1)}, u32[]{:S(2)}) copy-start(bf16[2,512,512]{2,1,0:T(8,128)(2,1)} %k_ref.5) | copy-start | bytes 3145732
  57.7 12.7 %copy-start.5 = (s32[2]{0:T(128)S(1)}, s32[2]{0:T(128)}, u32[]{:S(2)}) copy-start(s32[2]{0:T(128)} %len_ref.5) | copy-start | bytes 28
  58.6 10.5 %all-to-all-start.1 = ((bf16[32,2,4096]{2,0,1:T(8,128)(2,1)}), bf16[32,2,4096]{2,0,1:T(8,128)(2,1)S(1)}, u32[]{:S(2)}, u32[]{:S(2)}) async-start(bf16[32,2,4096]{2,0,1:T(8,128)(2,1)} %bitcast.26), calls=%async_computation.1 | async-start | bytes 1048576 | tf_op jit(solution)/shard_map/all_to_all | solution.py:302
  70.4 1.2 copy-start.3
  138.8 17.6 %all-to-all-start.2 = ((bf16[32,2,4096]{2,1,0:T(2,128)(2,1)}), bf16[32,2,4096]{2,1,0:T(2,128)(2,1)S(1)}, u32[]{:S(2)}, u32[]{:S(2)}) async-start(bf16[32,2,4096]{2,1,0:T(2,128)(2,1)} %all_to_all.42), calls=%async_computation.2 | async-start | bytes 1048576 | tf_op jit(solution)/shard_map/all_to_all | solution.py:327
  156.4 18.6 %all-to-all-start.3 = ((bf16[32,2,4096]{2,1,0:T(2,128)(2,1)}), bf16[32,2,4096]{2,1,0:T(2,128)(2,1)S(1)}, u32[]{:S(2)}, u32[]{:S(2)}) async-start(bf16[32,2,4096]{2,1,0:T(2,128)(2,1)} %all_to_all.44), calls=%async_computation.3 | async-start | bytes 1048576 | tf_op jit(solution)/shard_map/all_to_all | solution.py:327
  159.9 53.4 %all-gather.3.cloned.1.call-start = ((), (), s32[]{:S(2)}) async-start(), calls=%async_computation.4 | async-start | bytes 1114112 | tf_op jit(solution)/shard_map/all_gather | solution.py:333
Sparse Core Ops, SparseCore 0:
  176.3 36.9 all-gather.2
where the time goes:
time: 230 us; the launch traced here: 227 us
  waiting for transfers between devices  70.7 us (31%)
  Pallas kernels  56.9 us (25%)
  blocking collectives  50.4 us (22%)
  local copies, waits for them, and re-layouts  19 us (8%)
  between operations  14.2 us (6%)
  starting transfers between devices  14.1 us (6%)
    all_gather x1, blocking collectives, shards(): stats = lax.all_gather(stats, 'psg', axis=0)  50.4 us
    pallas_call x1, Pallas kernels, run_passages(): pl.pallas_call(functools.partial(passage_kernel, 0, False), grid=(count,...  41.4 us
    all_gather x1, waiting for transfers between devices, shards(): both = lax.all_gather(both, 'psg', axis=1, tiled=True)  37.1 us
    all_to_all x2, waiting for transfers between devices, to_owners(): lax.all_to_all(part, ('psg', 'row'), split_axis=0, concat_axis=0, tiled=T...  28.3 us
    pallas_call x1, Pallas kernels, run_grads(): pl.pallas_call(grads_kernel, grid=(kv,), in_specs=[pl.BlockSpec(memory_sp...  10.3 us
    all_to_all x2, starting transfers between devices, to_groups(): got = lax.all_to_all(rows, 'row', split_axis=1, concat_axis=0, tiled=True)  7.89 us
    unnamed x18, local copies, waits for them, and re-layouts  7.08 us
    all_to_all x2, starting transfers between devices, to_owners(): lax.all_to_all(part, ('psg', 'row'), split_axis=0, concat_axis=0, tiled=T...  6.15 us
  transfers between devices with their start and end apart: 5, of which 4 were waited for; matrix products, arithmetic and copies ran while one was open for 1% of the time, Pallas kernels for 18%

commit v1 on v0

--- a/solution.py
+++ b/solution.py
@@ -48,23 +48,17 @@
     return jnp.concatenate([ref_rows(h) for h in heads], axis=0)
 
 
-def passage_kernel(first, adds, len_ref, q_ref, k_ref, v_ref, g_ref, *rest):
-    if adds:
-        ak_ref, av_ref = rest[:2]
+def passage_kernel(index, len_ref, q_ref, k_ref, v_ref, g_ref, ak_ref, av_ref, *rest):
     o_ref, dq_ref, dk_ref, dv_ref, dk_acc, dv_acc = rest[-6:]
     slots = k_ref.shape[1]
     groups = q_ref.shape[2] // HEAD_SIZE
-    length = len_ref[first + pl.program_id(0)]
+    length = len_ref[index]
     key = k_ref[0]
     val = v_ref[0]
     key_t = key.T
     val_t = val.T
-    if adds:
-        dk_acc[...] = ak_ref[0]
-        dv_acc[...] = av_ref[0]
-    else:
-        dk_acc[...] = jnp.zeros_like(dk_acc)
-        dv_acc[...] = jnp.zeros_like(dv_acc)
+    dk_acc[...] = ak_ref[0]
+    dv_acc[...] = av_ref[0]
     width = 2 * BLOCK
     causal = lax.broadcasted_iota(jnp.int32, (BLOCK, width), 0) <= (
         lax.broadcasted_iota(jnp.int32, (BLOCK, width), 1) & (BLOCK - 1)
@@ -118,32 +112,35 @@
     dv_ref[0] = dv_acc[...].astype(dv_ref.dtype)
 
 
-def run_passages(lengths, query, key, val, grad):
+def run_passage(index, lengths, query, key, val, grad, ans_dk, ans_dv, before):
     count, slots, feat = query.shape
     kv = key.shape[2] // HEAD_SIZE
     group_width = feat // kv
-    wide = pl.BlockSpec((1, slots, group_width), lambda p, g: (p, 0, g))
-    thin = pl.BlockSpec((1, slots, HEAD_SIZE), lambda p, g: (p, 0, g))
+    wide = pl.BlockSpec((1, slots, group_width), lambda p, g: (index, 0, g))
+    thin = pl.BlockSpec((1, slots, HEAD_SIZE), lambda p, g: (index, 0, g))
+    kept = pl.BlockSpec(memory_space=pl.ANY)
     return pl.pallas_call(
-        functools.partial(passage_kernel, 0, False),
-        grid=(count, kv),
-        in_specs=[pl.BlockSpec(memory_space=pltpu.SMEM), wide, thin, thin, wide],
+        functools.partial(passage_kernel, index),
+        grid=(1, kv),
+        in_specs=[pl.BlockSpec(memory_space=pltpu.SMEM), wide, thin, thin, wide, thin, thin]
+        + [kept] * len(before),
         out_specs=[wide, wide, thin, thin],
         out_shape=[
             jax.ShapeDtypeStruct(query.shape, BF16),
             jax.ShapeDtypeStruct(query.shape, BF16),
-            jax.ShapeDtypeStruct(key.shape, F32),
-            jax.ShapeDtypeStruct(key.shape, F32),
+            jax.ShapeDtypeStruct(key.shape, BF16),
+            jax.ShapeDtypeStruct(key.shape, BF16),
         ],
+        input_output_aliases={7 + n: n for n in range(len(before))},
         scratch_shapes=[pltpu.VMEM((slots, HEAD_SIZE), F32)] * 2,
         compiler_params=pltpu.CompilerParams(vmem_limit_bytes=VMEM_LIMIT),
         cost_estimate=pl.CostEstimate(
-            flops=8 * count * slots * slots * feat,
-            bytes_accessed=8 * count * slots * feat,
-            transcendentals=count * slots * slots * feat // HEAD_SIZE,
-        ),
-        name="passages",
-    )(lengths, query, key, val, grad)
+            flops=16 * slots * slots * feat,
+            bytes_accessed=8 * slots * feat,
+            transcendentals=slots * slots * feat // HEAD_SIZE,
+        ),
+        name="passage",
+    )(lengths, query, key, val, grad, ans_dk, ans_dv, *before)
 
 
 def rotated(key, cos, sin):
@@ -214,7 +211,7 @@
 
 
 def grads_kernel(
-    len_ref, cos_ref, sin_ref, q_ref, g_ref, k_ref, v_ref, stat_ref, pk_ref, pv_ref,
+    len_ref, cos_ref, sin_ref, q_ref, g_ref, k_ref, v_ref, stat_ref,
     o_ref, dq_ref, dk_ref, dv_ref, dk_acc, dv_acc,
 ):
     count, slots = k_ref.shape[:2]
@@ -259,11 +256,11 @@
     for p in range(count):
         dk = dk_acc[p] * SCALE
         dk = dk * cos_ref[p] - pltpu.roll(dk, HEAD_SIZE // 2, 1) * sin_ref[p]
-        dk_ref[p] = (dk + pk_ref[p]).astype(dk_ref.dtype)
-        dv_ref[p] = (dv_acc[p] + pv_ref[p]).astype(dv_ref.dtype)
-
-
-def run_grads(lengths, cos, sin, query, grad, key, val, stats, pass_dk, pass_dv):
+        dk_ref[p] = dk
+        dv_ref[p] = dv_acc[p]
+
+
+def run_grads(lengths, cos, sin, query, grad, key, val, stats):
     count, slots, feat = key.shape
     kv = feat // HEAD_SIZE
     tokens, width = query.shape
@@ -277,14 +274,14 @@
         grid=(kv,),
         in_specs=[
             pl.BlockSpec(memory_space=pltpu.SMEM),
-            whole, whole, wide, wide, thin, thin, stat, thin, thin,
+            whole, whole, wide, wide, thin, thin, stat,
         ],
         out_specs=[wide, wide, thin, thin],
         out_shape=[
             jax.ShapeDtypeStruct(query.shape, BF16),
             jax.ShapeDtypeStruct(query.shape, BF16),
-            jax.ShapeDtypeStruct(key.shape, BF16),
-            jax.ShapeDtypeStruct(key.shape, BF16),
+            jax.ShapeDtypeStruct(key.shape, F32),
+            jax.ShapeDtypeStruct(key.shape, F32),
         ],
         scratch_shapes=[pltpu.VMEM((count, slots, HEAD_SIZE), F32)] * 2,
         compiler_params=pltpu.CompilerParams(vmem_limit_bytes=VMEM_LIMIT),
@@ -294,17 +291,16 @@
             transcendentals=count * slots * tokens * groups * kv,
         ),
         name="answer_grads",
-    )(lengths, cos, sin, query, grad, key, val, stats, pass_dk, pass_dv)
+    )(lengths, cos, sin, query, grad, key, val, stats)
 
 
 def shards(n_psg, n_row, psg_len, offsets, p_query, passage_key, passage_value, p_grad, a_query, a_grad):
-    def to_groups(rows):
-        got = lax.all_to_all(rows, "row", split_axis=1, concat_axis=0, tiled=True)
-        got = got.reshape(n_row, n_psg, -1, got.shape[1])
-        return jnp.transpose(got, (1, 0, 2, 3)).reshape(-1, got.shape[3])
-
-    queries = to_groups(a_query)
-    grads_in = to_groups(a_grad)
+    sent = jnp.concatenate([a_query, a_grad], axis=0)
+    sent = jnp.transpose(sent.reshape(sent.shape[0], n_row, -1), (1, 0, 2))
+    got = lax.all_to_all(sent, "row", split_axis=0, concat_axis=0, tiled=True)
+    got = got.reshape(n_row, 2, n_psg, -1, got.shape[2])
+    got = jnp.transpose(got, (1, 2, 0, 3, 4)).reshape(2, -1, got.shape[4])
+    queries, grads_in = got[0], got[1]
     tokens, width = queries.shape
     share = tokens // (n_psg * n_row)
 
@@ -316,21 +312,25 @@
 
     stats = run_stats(psg_len, cos, sin, queries, grads_in, passage_key, passage_value)
     stats = lax.all_gather(stats, "psg", axis=0)
-    p_out, p_dq, pass_dk, pass_dv = run_passages(
-        psg_len, p_query, passage_key, passage_value, p_grad
+    o_part, dq_part, ans_dk, ans_dv = run_grads(
+        psg_len, cos, sin, queries, grads_in, passage_key, passage_value, stats
     )
-    o_part, dq_part, p_dk, p_dv = run_grads(
-        psg_len, cos, sin, queries, grads_in, passage_key, passage_value, stats, pass_dk, pass_dv
-    )
-
-    def to_owners(part):
-        got = lax.all_to_all(part, ("psg", "row"), split_axis=0, concat_axis=0, tiled=True)
-        got = got.reshape(n_psg, n_row, share, width).astype(F32)
-        return jnp.sum(got, axis=0).astype(BF16)
-
-    both = jnp.stack([to_owners(o_part), to_owners(dq_part)])
-    both = jnp.transpose(both, (0, 2, 1, 3)).reshape(2, share, n_row * width)
-    both = lax.all_gather(both, "psg", axis=1, tiled=True)
+    parts = jnp.concatenate([o_part, dq_part], axis=1)
+    parts = lax.all_to_all(parts, ("psg", "row"), split_axis=0, concat_axis=0, tiled=True)
+
+    local_count = p_query.shape[0]
+    done = ()
+    for index in range(local_count):
+        done = run_passage(
+            index, psg_len, p_query, passage_key, passage_value, p_grad, ans_dk, ans_dv, done
+        )
+        if index == 0:
+            both = parts.reshape(n_psg, n_row, share, 2, width).astype(F32)
+            both = jnp.sum(both, axis=0).astype(BF16)
+            both, done = lax.optimization_barrier((both, tuple(done)))
+            both = jnp.transpose(both, (2, 1, 0, 3)).reshape(2, share, n_row * width)
+            both = lax.all_gather(both, "psg", axis=1, tiled=True)
+    p_out, p_dq, p_dk, p_dv = done
     return (p_out, p_dq, p_dk, p_dv, both[0], both[1])
 
 

time: 230 us -> 178 us (0.77); the launches traced: 227 us -> 177 us
  waiting for transfers between devices: 70.7 us -> 37.9 us
  blocking collectives: 50.4 us -> 22.6 us
  Pallas kernels: 56.9 us -> 69.6 us
  starting transfers between devices: 14.1 us -> 7.07 us
  other arithmetic: 1.26 us -> 4.83 us
    all_gather x1, blocking collectives: 50.4 us -> 22.6 us  [shards(): stats = lax.all_gather(stats, 'psg', axis=0)]
    all_to_all x4 -> x2, waiting for transfers between devices: 33.6 us -> 14.2 us  [the longest x1 14.2 us: shards(): got = lax.all_to_all(sent, 'row', split_axis=0, concat_axis=0, tiled=True)]
    all_gather x1, waiting for transfers between devices: 37.1 us -> 23.7 us  [shards(): both = lax.all_gather(both, 'psg', axis=1, tiled=True)]
    pallas_call x1 -> x2, Pallas kernels: 41.4 us -> 54.2 us  [run_passage(): pl.pallas_call(functools.partial(passage_kernel, index), grid=(1, kv), in...]
    all_to_all x4 -> x2, starting transfers between devices: 14 us -> 6.85 us  [the longest x1 4.21 us: shards(): got = lax.all_to_all(sent, 'row', split_axis=0, concat_axis=0, tiled=True)]
    slice x0 -> x3, local copies, waits for them, and re-layouts: none -> 4.64 us  [shards(): queries, grads_in = (got[0], got[1])]
    unnamed x18 -> x12, local copies, waits for them, and re-layouts: 7.08 us -> 2.77 us
    all_to_all x6 -> x2, local copies, waits for them, and re-layouts: 6.04 us -> 3.71 us  [the longest x1 2.62 us: shards(): lax.all_to_all(parts, ('psg', 'row'), split_axis=0, concat_axis=0, tiled=...]
  transfers between devices with their start and end apart: 5 -> 3, of which waited for: 4 -> 2; matrix products, arithmetic and copies ran while one was open for 1% -> 0% of each run, Pallas kernels for 18% -> 31%
where the time goes in v1:
time: 178 us; the launch traced here: 177 us
  Pallas kernels  69.6 us (39%)
  waiting for transfers between devices  37.9 us (21%)
  blocking collectives  22.6 us (13%)
  local copies, waits for them, and re-layouts  20.8 us (12%)
  between operations  14.1 us (8%)
  starting transfers between devices  7.07 us (4%)
  other arithmetic  4.83 us (3%)
    pallas_call x2, Pallas kernels, run_passage(): pl.pallas_call(functools.partial(passage_kernel, index), grid=(1, kv), in...  54.2 us
    all_gather x1, waiting for transfers between devices, shards(): both = lax.all_gather(both, 'psg', axis=1, tiled=True)  23.7 us
    all_gather x1, blocking collectives, shards(): stats = lax.all_gather(stats, 'psg', axis=0)  22.6 us
    all_to_all x1, waiting for transfers between devices, shards(): got = lax.all_to_all(sent, 'row', split_axis=0, concat_axis=0, tiled=True)  14.2 us
    pallas_call x1, Pallas kernels, run_grads(): pl.pallas_call(grads_kernel, grid=(kv,), in_specs=[pl.BlockSpec(memory_sp...  10.1 us
    pallas_call x1, Pallas kernels, run_stats(): pl.pallas_call(stats_kernel, grid=(kv,), in_specs=[pl.BlockSpec(memory_sp...  5.28 us
    slice x3, local copies, waits for them, and re-layouts, shards(): queries, grads_in = (got[0], got[1])  4.64 us
    all_to_all x1, starting transfers between devices, shards(): got = lax.all_to_all(sent, 'row', split_axis=0, concat_axis=0, tiled=True)  4.21 us
  transfers between devices with their start and end apart: 3, of which 2 were waited for; matrix products, arithmetic and copies ran while one was open for 0% of the time, Pallas kernels for 31%

profile of v1, /device:TPU:0, one launch (start us, length us, event | category | flops | bytes accessed | tf_op | source)
XLA Modules:
  0.0 177.0 jit_solution(17589279411497931291)
XLA Ops:
  7.2 1.3 pad_maximum_fusion
  8.4 0.8 reshape.179
  9.3 1.6 copy.23
  10.8 4.2 %all-to-all-start = ((bf16[2,64,4096]{2,1,0:T(8,128)(2,1)}), bf16[2,64,4096]{2,1,0:T(8,128)(2,1)S(1)}, u32[]{:S(2)}, u32[]{:S(2)}) async-start(bf16[2,64,4096]{2,1,0:T(8,128)(2,1)} %copy.23), calls=%async_computation | async-start | bytes 2097152 | tf_op jit(solution)/shard_map/all_to_all | solution.py:300
  15.2 14.2 %all-to-all-done = bf16[2,64,4096]{2,1,0:T(8,128)(2,1)S(1)} async-done(((bf16[2,64,4096]{2,1,0:T(8,128)(2,1)}), bf16[2,64,4096]{2,1,0:T(8,128)(2,1)S(1)}, u32[]{:S(2)}, u32[]{:S(2)}) %all-to-all-start) | async-done | bytes 1048608 | tf_op jit(solution)/shard_map/all_to_all | solution.py:300
  29.5 1.1 copy.24
  30.5 1.7 fusion.2
  33.0 2.4 %copy.25 = bf16[1,16,2,2,4096]{4,3,2,1,0:T(2,128)(2,1)} copy(bf16[1,16,2,2,4096]{4,2,3,1,0:T(2,128)(2,1)} %get-tuple-element.45) | data formatting | bytes 1048576 | tf_op jit(solution)/shard_map/slice | solution.py:303
  35.4 1.2 squeeze.12.q_ref
  36.7 5.3 %answer_stats.1 = f32[4,2,512]{2,1,0:T(2,128)S(1)} custom-call(s32[2]{0:T(128)S(1)} %copy-done.3, f32[2,1,128]{2,1,0:T(1,128)S(1)} %get-tuple-element.47.cos_ref, f32[2,1,128]{2,1,0:T(1,128)S(1)} %get-tuple-element.48.sin_ref, bf16[64,4096]{1,0:T(8,128)(2,1)S(1)} %squeeze.12.q_ref, bf16[64,4096]{1,0:T(8,128)(2,1)S(1)} %squeeze.13.g_ref, ...), custom_call_target="tpu_custom_call" | custom-call | flops 1073741824 | bytes 3145728 | tf_op jit(solution)/shard_map/answer_stats/pallas_call | solution.py:197
  42.0 22.6 %all-gather = f32[64,2,512]{2,1,0:T(2,128)S(1)} all-gather(f32[4,2,512]{2,1,0:T(2,128)S(1)} %answer_stats.1), channel_id=2, replica_groups=mesh['psg'=16,'row'=2] {'psg'}, dimensions={0}, use_global_device_ids=true | all-gather | bytes 278528 | tf_op jit(solution)/shard_map/all_gather | solution.py:314
  64.6 10.1 %answer_grads.1 = (bf16[64,4096]{1,0:T(8,128)(2,1)S(1)}, bf16[64,4096]{1,0:T(8,128)(2,1)S(1)}, f32[2,512,512]{2,1,0:T(8,128)}, f32[2,512,512]{2,1,0:T(8,128)}) custom-call(s32[2]{0:T(128)S(1)} %copy-done.3, f32[2,1,128]{2,1,0:T(1,128)S(1)} %get-tuple-element.47.cos_ref, f32[2,1,128]{2,1,0:T(1,128)S(1)} %get-tuple-element.48.sin_ref, ...), custom_call_target="tpu_custom_call" | custom-call | flops 3221225472 | bytes 10485760 | tf_op jit(solution)/shard_map/answer_grads/pallas_call | solution.py:272
  74.7 1.0 pad_maximum_fusion.1
  75.8 2.6 %all_to_all.10 = bf16[32,2,8192]{2,1,0:T(2,128)(2,1)} reshape(bf16[64,8192]{1,0:T(8,128)(2,1)} %pad_maximum_fusion.1) | data formatting | bytes 2097152 | tf_op jit(solution)/shard_map/all_to_all | solution.py:319
  78.4 2.6 %all-to-all-start.1 = ((bf16[32,2,8192]{2,1,0:T(2,128)(2,1)}), bf16[32,2,8192]{2,1,0:T(2,128)(2,1)S(1)}, u32[]{:S(2)}, u32[]{:S(2)}) async-start(bf16[32,2,8192]{2,1,0:T(2,128)(2,1)} %all_to_all.10), calls=%async_computation.1 | async-start | bytes 2097152 | tf_op jit(solution)/shard_map/all_to_all | solution.py:319
  81.3 27.0 %passage.2 = (bf16[2,512,4096]{2,1,0:T(8,128)(2,1)}, bf16[2,512,4096]{2,1,0:T(8,128)(2,1)}, bf16[2,512,512]{2,1,0:T(8,128)(2,1)}, bf16[2,512,512]{2,1,0:T(8,128)(2,1)}) custom-call(s32[2]{0:T(128)S(1)} %copy-done.3, bf16[2,512,4096]{2,1,0:T(8,128)(2,1)} %q_ref.3, bf16[2,512,512]{2,1,0:T(8,128)(2,1)S(1)} %copy-done, bf16[2,512,512]{2,1,0:T(8,128)(2,1)S(1)} %copy-done.2, ...), custom_call_target="tpu_custom_call" | custom-call | flops 17179869184 | bytes 16777216 | tf_op jit(solution)/shard_map/passage/pallas_call | solution.py:122
  108.3 1.6 reshape.181
  109.9 2.3 %reduce_sum.12 = bf16[2,2,2,4096]{3,2,1,0:T(2,128)(2,1)S(1)} reduce(bf16[16,2,2,2,4096]{4,3,2,1,0:T(2,128)(2,1)} %reshape.181, bf16[]{:T(256)} %constant.23.clone.1), dimensions={0}, to_apply=%region_0.1 | reduce | flops 491520 | bytes 1114114 | tf_op jit(solution)/shard_map/reduce_sum | solution.py:329
  112.2 0.7 copy.35
  112.9 27.2 %passage.3 = (bf16[2,512,4096]{2,1,0:T(8,128)(2,1)}, bf16[2,512,4096]{2,1,0:T(8,128)(2,1)}, bf16[2,512,512]{2,1,0:T(8,128)(2,1)}, bf16[2,512,512]{2,1,0:T(8,128)(2,1)}) custom-call(s32[2]{0:T(128)S(1)} %copy-done.3, bf16[2,512,4096]{2,1,0:T(8,128)(2,1)} %q_ref.3, ...), custom_call_target="tpu_custom_call", output_to_operand_aliasing={{0}: (7, {}), {1}: (8, {}), {2}: (9, {}), {3}: (10, {})} | custom-call | flops 17179869184 | bytes 16777216 | tf_op jit(solution)/shard_map/passage/pallas_call | solution.py:122
  140.1 23.7 %all-gather.3.cloned.1.call-done = bf16[2,32,8192]{2,0,1:T(2,128)(2,1)} async-done(((bf16[2,2,8192]{2,0,1:T(2,128)(2,1)}), bf16[2,32,8192]{2,0,1:T(2,128)(2,1)}) %all-gather.3.cloned.1.call-update) | async-done | bytes 1048592 | tf_op jit(solution)/shard_map/all_gather | solution.py:332
  163.8 3.6 %fusion.1 = (bf16[1,32,8192]{2,0,1:T(2,128)(2,1)S(1)}, bf16[1,32,8192]{2,0,1:T(2,128)(2,1)S(1)}) fusion(bf16[2,32,8192]{2,0,1:T(2,128)(2,1)} %all-gather.3.cloned.1.call-done), kind=kLoop, calls=%fused_computation.11 | loop fusion | bytes 2097152 | tf_op jit(solution)/shard_map/slice | solution.py:334
  167.4 1.4 copy.38
  168.8 1.4 copy.39
  (19 shorter events, 1.2 us)
Async XLA Ops:
  9.2 5.8 %copy-start.4 = (s32[2]{0:T(128)S(1)}, s32[2]{0:T(128)}, u32[]{:S(2)}) copy-start(s32[2]{0:T(128)} %param.9) | copy-start | bytes 28
  10.8 18.6 %all-to-all-start = ((bf16[2,64,4096]{2,1,0:T(8,128)(2,1)}), bf16[2,64,4096]{2,1,0:T(8,128)(2,1)S(1)}, u32[]{:S(2)}, u32[]{:S(2)}) async-start(bf16[2,64,4096]{2,1,0:T(8,128)(2,1)} %copy.23), calls=%async_computation | async-start | bytes 2097152 | tf_op jit(solution)/shard_map/all_to_all | solution.py:300
  32.3 4.4 %copy-start = (bf16[2,512,512]{2,1,0:T(8,128)(2,1)S(1)}, bf16[2,512,512]{2,1,0:T(8,128)(2,1)}, u32[]{:S(2)}) copy-start(bf16[2,512,512]{2,1,0:T(8,128)(2,1)} %k_ref.7) | copy-start | bytes 3145732
  32.3 4.4 %copy-start.1 = (bf16[2,512,512]{2,1,0:T(8,128)(2,1)S(1)}, bf16[2,512,512]{2,1,0:T(8,128)(2,1)}, u32[]{:S(2)}) copy-start(bf16[2,512,512]{2,1,0:T(8,128)(2,1)} %v_ref.7) | copy-start | bytes 3145732
  32.3 4.4 %copy-start.3 = (s32[2]{0:T(128)S(1)}, s32[2]{0:T(128)}, u32[]{:S(2)}) copy-start(s32[2]{0:T(128)} %len_ref.7) | copy-start | bytes 28
  75.8 5.5 %copy-start.2 = (bf16[2,512,512]{2,1,0:T(8,128)(2,1)S(1)}, bf16[2,512,512]{2,1,0:T(8,128)(2,1)}, u32[]{:S(2)}) copy-start(bf16[2,512,512]{2,1,0:T(8,128)(2,1)} %v_ref.7) | copy-start | bytes 3145732
  78.4 29.9 %all-to-all-start.1 = ((bf16[32,2,8192]{2,1,0:T(2,128)(2,1)}), bf16[32,2,8192]{2,1,0:T(2,128)(2,1)S(1)}, u32[]{:S(2)}, u32[]{:S(2)}) async-start(bf16[32,2,8192]{2,1,0:T(2,128)(2,1)} %all_to_all.10), calls=%async_computation.1 | async-start | bytes 2097152 | tf_op jit(solution)/shard_map/all_to_all | solution.py:319
  81.0 82.7 %all-gather.3.cloned.1.call-start = ((), (), s32[]{:S(2)}) async-start(), calls=%async_computation.2 | async-start | bytes 1114112 | tf_op jit(solution)/shard_map/all_gather | solution.py:332
Sparse Core Ops, SparseCore 0:
  113.0 50.7 all-gather.2
